TPU v7x, 512 devices: a whole 4x8x8 slice. The times are simulated.
512 devices in a mesh: row: 16 (over y_hi, x), col: 32 (over z, y_lo, core).
Axes of the slice: x: 4, y: 8 (y_hi: 4, y_lo: 2; y = y_hi * 2 + y_lo), z: 8, core: 2. Of those that a mesh axis runs over, the one named last changes fastest.
Arguments:
- hidden_act: bfloat16 [2048, 28672], P('row', 'col'), may hold values from -0.14941406 to 0.14941406
- out_grad: bfloat16 [2048, 8192], P('col', 'row'), may hold values from -6 to 6
- weight: bfloat16 [28672, 8192], P('col', 'row'), may hold values from -0.03125 to 0.03125
- loss_mask: int32 [2048], replicated, may hold values from 0 to 1
- positions: int32 [2048], replicated, may hold values from 0 to 255, as said below
Outputs:
- input_grad: bfloat16 [2048, 28672], P('row', 'col')
- weight_grad: bfloat16 [28672, 8192], P('col', 'row')
Inputs may be any that keep to these rules, and one draw needn't show every extreme that they name: positions is 0 at the first token and otherwise either 0 or one more than the previous token's; no document is longer than min(512, 256) tokens.
All inputs are finite; a program needn't handle non-finite values.
Results may differ from a plain program's by a relative error of at most 0.019.
Values may be sent and summed in bfloat16 or wider, within the bound.
A program may use at most 64 MiB of HBM per device.

v0:
```python
import jax
import jax.numpy as jnp
from jax import lax
from jax.sharding import PartitionSpec as P


def token_weights(loss_mask, positions):
    count_all = positions.shape[0]
    indices = jnp.arange(count_all, dtype=jnp.int32)
    doc_first = indices - positions
    boundary = jnp.where(positions == 0, indices, count_all)
    following = jnp.concatenate([boundary[1:], jnp.full((1,), count_all, jnp.int32)])
    doc_end = lax.cummin(following, axis=0, reverse=True)
    kept_prefix = jnp.concatenate([jnp.zeros((1,), jnp.int32), jnp.cumsum(loss_mask)])
    kept_counts = jnp.maximum(kept_prefix[doc_end] - kept_prefix[doc_first], 1)
    doc_lengths = doc_end - doc_first
    return (
        loss_mask.astype(jnp.float32)
        * doc_lengths.astype(jnp.float32)
        / kept_counts.astype(jnp.float32)
    )


def on_device(hidden_act, out_grad, weight, loss_mask, positions):
    token_scale = token_weights(loss_mask, positions)
    local_rows = out_grad.shape[0]
    col_index = lax.axis_index("col")
    local_scale = lax.dynamic_slice_in_dim(token_scale, col_index * local_rows, local_rows, 0)
    scaled_local = (out_grad.astype(jnp.float32) * local_scale[:, None]).astype(jnp.bfloat16)
    scaled_all = lax.all_gather(scaled_local, "col", axis=0, tiled=True)
    partial_sum = lax.dot_general(
        scaled_all, weight, (((1,), (1,)), ((), ())), preferred_element_type=jnp.float32
    )
    summed = lax.psum_scatter(
        partial_sum.astype(jnp.bfloat16), "row", scatter_dimension=0, tiled=True
    )
    gathered = lax.all_gather(hidden_act, "row", axis=0, tiled=True)
    weight_sum = lax.dot_general(
        gathered, scaled_all, (((0,), (0,)), ((), ())), preferred_element_type=jnp.float32
    )
    return (summed, weight_sum.astype(jnp.bfloat16))


def solution(mesh):
    return jax.shard_map(
        on_device,
        mesh=mesh,
        in_specs=(P("row", "col"), P("col", "row"), P("col", "row"), P(), P()),
        out_specs=(P("row", "col"), P("col", "row")),
        check_vma=False,
    )
```

profile of v0, /device:TPU:1, one launch (start us, length us, event | category | flops | bytes accessed | tf_op | source)
XLA Modules:
  0.0 299.3 jit_solution(1510943413100434939)
XLA Ops:
  7.2 0.0 copy-start
  7.2 0.0 all-gather.3.cloned.1.call-start
  7.2 0.8 add_select_fusion
  8.1 0.1 add_bitcast_fusion
  8.1 2.3 reduce-window.16
  10.5 0.1 reduce-window.19
  10.5 0.1 slice_reduce_fusion.1
  10.6 0.1 fusion.10
  10.7 0.1 broadcast_minimum_fusion
  10.8 0.7 fusion.1
  11.5 1.0 reduce-window.24
  12.5 0.1 slice.29
  12.6 0.1 slice_reduce_fusion
  12.7 0.1 add_bitcast_fusion.1
  12.8 0.1 pad_add_fusion
  12.9 11.8 %gather_fusion = s32[2048]{0:T(1024)S(1)} fusion(s32[2049]{0:T(1024)S(1)} %pad_add_fusion, s32[2048]{0:T(1024)S(1)} %broadcast_clamp_fusion), kind=kCustom, calls=%fused_computation | custom fusion | bytes 24576 | tf_op jit(solution)/shard_map/gather | solution.py:15
  24.7 0.0 copy-start.1
  24.7 11.8 %gather_fusion.1 = s32[2048]{0:T(1024)S(1)} fusion(s32[2049]{0:T(1024)S(1)} %pad_add_fusion, s32[2048]{0:T(1024)S(1)} %get-tuple-element.6), kind=kCustom, calls=%fused_computation.1 | custom fusion | bytes 24576 | tf_op jit(solution)/shard_map/gather | solution.py:15
  36.5 0.8 fusion.3
  37.3 0.0 copy-done.1
  37.3 0.7 multiply_convert_fusion
  38.0 0.0 all-gather.3.cloned.1.call-update
  38.0 0.0 all-gather.5.cloned.1.call-start
  38.0 0.7 all-gather.5.cloned.1.call-update
  38.7 0.0 reduce-scatter.2.cloned.1.call-start
  38.8 73.1 %all-gather.3.cloned.1.call-done = bf16[2048,512]{1,0:T(8,128)(2,1)} async-done(((bf16[64,512]{1,0:T(8,128)(2,1)}), bf16[2048,512]{1,0:T(8,128)(2,1)}) %all-gather.3.cloned.1.call-update) | async-done | bytes 2097168 | tf_op jit(solution)/shard_map/all_gather | solution.py:30
  111.9 5.8 %convolution_convert_fusion = bf16[2048,896]{1,0:T(8,128)(2,1)} fusion(bf16[2048,512]{1,0:T(8,128)(2,1)} %all-gather.3.cloned.1.call-done, bf16[896,512]{1,0:T(8,128)(2,1)S(1)} %copy-done), kind=kOutput, calls=%fused_computation.2 | convolution fusion | flops 1880883200 | bytes 6684672 | tf_op jit(solution)/shard_map/dot_general | solution.py:31
  117.7 0.0 reduce-scatter.2.cloned.1.call-update
  117.7 71.1 %all-gather.5.cloned.1.call-done = bf16[2048,896]{1,0:T(8,128)(2,1)} async-done(((bf16[128,896]{1,0:T(8,128)(2,1)}), bf16[2048,896]{1,0:T(8,128)(2,1)}) %all-gather.5.cloned.1.call-update) | async-done | bytes 3670032 | tf_op jit(solution)/shard_map/all_gather | solution.py:37
  188.8 5.0 %fusion = bf16[896,512]{0,1:T(8,128)(2,1)S(1)} fusion(bf16[2048,512]{1,0:T(8,128)(2,1)} %all-gather.3.cloned.1.call-done, bf16[2048,896]{1,0:T(8,128)(2,1)} %all-gather.5.cloned.1.call-done), kind=kOutput, calls=%fused_computation.4 | convolution fusion | flops 1879506944 | bytes 6684672 | tf_op jit(solution)/shard_map/dot_general | solution.py:38
  193.8 1.3 copy.8
  195.1 97.7 %reduce-scatter.2.cloned.1.call-done = bf16[128,896]{1,0:T(8,128)(2,1)} async-done(((bf16[2048,896]{1,0:T(8,128)(2,1)}), bf16[128,896]{1,0:T(8,128)(2,1)}) %reduce-scatter.2.cloned.1.call-update) | async-done | bytes 229392 | tf_op jit(solution)/shard_map/reduce_scatter | solution.py:34
  (4 shorter events, 0.1 us)
Async XLA Ops:
  7.2 104.7 %copy-start = (bf16[896,512]{1,0:T(8,128)(2,1)S(1)}, bf16[896,512]{1,0:T(8,128)(2,1)}, u32[]{:S(2)}) copy-start(bf16[896,512]{1,0:T(8,128)(2,1)} %param.7) | copy-start | bytes 2752516
  7.2 104.7 %all-gather.3.cloned.1.call-start = ((), (), s32[]{:S(2)}) async-start(), calls=%async_computation.1 | async-start | bytes 2162688 | tf_op jit(solution)/shard_map/all_gather | solution.py:30
  24.7 12.6 %copy-start.1 = (bf16[64,512]{1,0:T(8,128)(2,1)S(1)}, bf16[64,512]{1,0:T(8,128)(2,1)}, u32[]{:S(2)}) copy-start(bf16[64,512]{1,0:T(8,128)(2,1)} %param.6) | copy-start | bytes 196612
  38.0 150.8 %all-gather.5.cloned.1.call-start = ((), (), s32[]{:S(2)}) async-start(), calls=%async_computation.3 | async-start | bytes 3899392 | tf_op jit(solution)/shard_map/all_gather | solution.py:37
  38.7 254.0 %reduce-scatter.2.cloned.1.call-start = ((), (), s32[]{:S(2)}) async-start(), calls=%async_computation.2 | async-start | bytes 3899392 | tf_op jit(solution)/shard_map/reduce_scatter | solution.py:34
Sparse Core Ops, SparseCore 0:
  38.1 73.7 all-gather.2
  114.9 73.8 all-gather.4
  193.6 99.1 reduce-scatter.1
where the time goes:
time: 300 us; the launch traced here: 299 us
  waiting for transfers between devices  243 us (81%)
  local copies, waits for them, and re-layouts  25.2 us (8%)
  between operations  13.8 us (5%)
  matrix products  10.8 us (4%)
  other arithmetic  6.82 us (2%)
    reduce_scatter x1, waiting for transfers between devices, on_device(): lax.psum_scatter(partial_sum.astype(jnp.bfloat16), 'row', scatter_dimensi...  97.7 us
    all_gather x1, waiting for transfers between devices, on_device(): scaled_all = lax.all_gather(scaled_local, 'col', axis=0, tiled=True)  73.1 us
    all_gather x1, waiting for transfers between devices, on_device(): gathered = lax.all_gather(hidden_act, 'row', axis=0, tiled=True)  71.1 us
    gather x2, local copies, waits for them, and re-layouts, token_weights(): kept_counts = jnp.maximum(kept_prefix[doc_end] - kept_prefix[doc_first], 1)  23.6 us
  transfers between devices with their start and end apart: 3, of which 3 were waited for; matrix products, arithmetic and copies ran while one was open for 4% of the time, Pallas kernels for 0%

commit v1 on v0

v1 whole, which is shorter than its diff:
```python
import jax
import jax.numpy as jnp
from jax import lax
from jax.experimental import pallas as pl
from jax.experimental.pallas import tpu as pltpu
from jax.sharding import PartitionSpec as P

MESH = pl.DeviceIdType.MESH
BF16 = jnp.bfloat16
F32 = jnp.float32
NY, NX, NZ = 4, 4, 8
CH = 4


def local_token_scale(mask_ref, pos_ref, col, n_local):
    rows = pos_ref.shape[0]
    lane = lax.broadcasted_iota(jnp.int32, (n_local, 128), 1)
    sub = lax.broadcasted_iota(jnp.int32, (n_local, 128), 0)
    per = 128 // n_local
    mine_row = col // per
    offset = (col % per) * n_local
    pick = lane == sub + offset
    mine_pos = pos_ref[pl.ds(mine_row, 1), :]
    mine_mask = mask_ref[pl.ds(mine_row, 1), :]
    first = jnp.sum(jnp.where(pick, (mine_row * 128 + lane - mine_pos).astype(F32), 0.0), axis=1, keepdims=True)
    own_mask = jnp.sum(jnp.where(pick, mine_mask.astype(F32), 0.0), axis=1, keepdims=True)
    length = jnp.zeros((n_local, 128), F32)
    kept = jnp.zeros((n_local, 128), F32)
    for q in range(rows):
        begins = (q * 128 + lane - pos_ref[q : q + 1, :]).astype(F32)
        same = begins == first
        length = length + jnp.where(same, 1.0, 0.0)
        kept = kept + jnp.where(same, mask_ref[q : q + 1, :].astype(F32), 0.0)
    length = jnp.sum(length, axis=1, keepdims=True)
    kept = jnp.maximum(jnp.sum(kept, axis=1, keepdims=True), 1.0)
    return own_mask * length / kept


def dot_nn(a, b):
    return lax.dot_general(a, b, (((1,), (0,)), ((), ())), preferred_element_type=F32)


def dot_nt(a, b):
    return lax.dot_general(a, b, (((1,), (1,)), ((), ())), preferred_element_type=F32)


def kernel(
    hid_ref, og_ref, w_ref, mask_ref, pos_ref, ig_ref, wg_ref,
    sc, hidt, S, wrecv, wg_send, wg_recv, wg_own, ig_send, ig_recv, ig_own, igy_send, igy_recv,
    sc_s, sc_r, hy_s, hy_r, hx_s, hx_r, w_s, w_r, z_s, z_r, k_s, k_r, wg_s, wg_r, ig_s, ig_r, iy_s, iy_r,
):
    row = lax.axis_index("row")
    col = lax.axis_index("col")
    Y, x = row // NX, row % NX
    z, l, k = col // 4, (col // 2) % 2, col % 2
    dpx = x + 1 - 2 * (x % 2)
    tpx = 3 - x
    par, tpar = x // 2, 1 - x // 2
    g = ((x + 1) // 2) % 2
    lt = (z % 2 + g) % 2

    def dev(Y=Y, x=x, z=z, l=l, k=k):
        return (Y * NX + x, z * 4 + l * 2 + k)

    dp, tp, other = dev(x=dpx), dev(x=tpx), dev(k=1 - k)
    zdev = (dev(z=(z + 1) % NZ), dev(z=(z + NZ - 1) % NZ))
    ydev = [dev(Y=(Y + d) % NY) for d in range(NY)]
    ldev, dpl = dev(l=1 - l), dev(x=dpx, l=1 - l)

    bar = pltpu.get_barrier_semaphore()
    peers = [dp, tp, other, *zdev, *ydev[1:], ldev, dpl]
    for p in peers:
        pl.semaphore_signal(bar, inc=1, device_id=p, device_id_type=MESH)

    def rc(src, dst, ss, rs, to):
        return pltpu.make_async_remote_copy(src, dst, ss, rs, device_id=to, device_id_type=MESH)

    scale = local_token_scale(mask_ref, pos_ref, col, og_ref.shape[0])
    sc[...] = (og_ref[...].astype(F32) * scale).astype(BF16)
    myj = 2 * Y + par
    hidt[myj] = hid_ref[...].T

    pl.semaphore_wait(bar, len(peers))

    member = l == lt
    a_far = rc(sc, S.at[z, k, 1], sc_s.at[0], sc_r.at[1], dp)
    b_far = rc(sc, S.at[z, k, 1], sc_s.at[1], sc_r.at[1], dpl)
    b_near = rc(sc, S.at[z, k, 0], sc_s.at[1], sc_r.at[0], ldev)

    @pl.when(member)
    def _():
        b_near.start()
        S[z, k, 0] = sc[...]

    @pl.when(jnp.logical_not(member))
    def _():
        a_far.start()
        b_far.start()

    hy = [rc(hidt.at[myj], hidt.at[myj], hy_s.at[d], hy_r.at[d], ydev[d]) for d in range(1, NY)]
    hx = [None] * NY

    def send_hx(d):
        j = 2 * ((Y + NY - d) % NY) + par
        hx[d] = rc(hidt.at[j], hidt.at[j], hx_s.at[d], hx_r.at[d], tp)
        hx[d].start()

    wc = rc(w_ref, wrecv, w_s.at[0], w_r.at[0], dp)
    hy[0].start()
    hy[2].start()
    send_hx(0)
    hy[1].start()
    wc.start()

    @pl.when(jnp.logical_not(member))
    def _():
        b_near.wait_recv()

    a_far.wait_recv()

    kc = []

    def to_core(zz, slot, idx):
        c = rc(S.at[zz, k, slot], S.at[zz, k, slot], k_s.at[idx], k_r.at[idx], other)
        c.start()
        kc.append(c)

    zc = {}

    def z_send(direction, step, slot):
        origin = (z + NZ - step) % NZ if direction == 0 else (z + step) % NZ
        i = (direction * 4 + step) * 2 + slot
        c = rc(S.at[origin, k, slot], S.at[origin, k, slot], z_s.at[i], z_r.at[i], zdev[direction])
        c.start()
        zc[direction, step, slot] = c

    for slot in range(2):
        for direction in range(2):
            z_send(direction, 0, slot)
    for slot in range(2):
        to_core(z, slot, slot)
    n = 2
    for step in range(1, 5):
        for slot in range(2):
            for direction in range(2):
                if step == 4 and slot != direction:
                    continue
                zc[direction, step - 1, slot].wait_recv()
                if step < 3 or (step == 3 and slot == direction):
                    z_send(direction, step, slot)
                origin = (z + NZ - step) % NZ if direction == 0 else (z + step) % NZ
                to_core(origin, slot, n)
                n += 1
        if step == 2:
            hy[0].wait_recv()
            send_hx(1)
            hy[2].wait_recv()
            send_hx(3)
    hy[1].wait_recv()
    send_hx(2)
    for c in kc:
        c.wait_recv()
    wc.wait_recv()

    def ig_block(d, parity):
        zz = 2 * ((Y + d) % NY) + parity
        s0 = S[zz, :, 0].reshape(128, -1)
        s1 = S[zz, :, 1].reshape(128, -1)
        return dot_nt(s0, w_ref[...]) + dot_nt(s1, wrecv[...])

    order = (2, 1, 3, 0)
    igc = {}
    for d in order:
        ig_send[d] = ig_block(d, tpar).astype(BF16)
        igc[d] = rc(ig_send.at[d], ig_recv.at[d], ig_s.at[d], ig_r.at[d], tp)
        igc[d].start()

    for d in range(NY):
        hx[d].wait_recv()
    rows = hid_ref.shape[1] // CH
    wgc = []

    def lhs(c):
        return jnp.concatenate([hidt[j, c * rows : (c + 1) * rows] for j in range(2 * NY)], axis=1)

    def rhs(slot):
        return S[:, :, slot].reshape(1024, -1)

    for c in range(CH):
        sl = pl.ds(c * rows, rows)
        wg_send[sl] = dot_nn(lhs(c), rhs(1)).astype(BF16)
        cp = rc(wg_send.at[sl], wg_recv.at[sl], wg_s.at[c], wg_r.at[c], dp)
        cp.start()
        wgc.append(cp)
    for d in order:
        ig_own[d] = ig_block(d, par)
    for c in range(CH):
        wg_own[c * rows : (c + 1) * rows] = dot_nn(lhs(c), rhs(0))

    iyc = {}
    for d in order:
        igc[d].wait_recv()
        total = ig_own[d] + ig_recv[d].astype(F32)
        if d:
            igy_send[d] = total.astype(BF16)
            iyc[d] = rc(igy_send.at[d], igy_recv.at[d], iy_s.at[d], iy_r.at[d], ydev[d])
            iyc[d].start()
        else:
            ig_own[0] = total
    for c in range(CH):
        wgc[c].wait_recv()
        sl = pl.ds(c * rows, rows)
        wg_ref[sl] = (wg_own[sl] + wg_recv[sl].astype(F32)).astype(BF16)
    for d in (1, 3, 2):
        iyc[d].wait_recv()
    ig_ref[...] = (
        ig_own[0] + igy_recv[1].astype(F32) + igy_recv[2].astype(F32) + igy_recv[3].astype(F32)
    ).astype(BF16)

    b_near.wait_send()

    @pl.when(jnp.logical_not(member))
    def _():
        a_far.wait_send()

    for c in [*hy, *hx, wc, *zc.values(), *kc, *igc.values(), *wgc, *iyc.values()]:
        c.wait_send()


def on_device(hidden_act, out_grad, weight, loss_mask, positions):
    t, f = hidden_act.shape
    n, b = out_grad.shape
    dma = pltpu.SemaphoreType.DMA
    vm = pltpu.VMEM
    return pl.pallas_call(
        kernel,
        out_shape=(jax.ShapeDtypeStruct((t, f), BF16), jax.ShapeDtypeStruct((f, b), BF16)),
        in_specs=[pl.BlockSpec(memory_space=vm)] * 5,
        out_specs=[pl.BlockSpec(memory_space=vm)] * 2,
        scratch_shapes=[
            vm((n, b), BF16),
            vm((8, f, t), BF16),
            vm((NZ, 2, 2, n, b), BF16),
            vm((f, b), BF16),
            vm((f, b), BF16),
            vm((f, b), BF16),
            vm((f, b), F32),
            vm((NY, t, f), BF16),
            vm((NY, t, f), BF16),
            vm((NY, t, f), F32),
            vm((NY, t, f), BF16),
            vm((NY, t, f), BF16),
            dma((2,)), dma((2,)),
            dma((4,)), dma((4,)),
            dma((4,)), dma((4,)),
            dma((1,)), dma((1,)),
            dma((16,)), dma((16,)),
            dma((16,)), dma((16,)),
            dma((CH,)), dma((CH,)),
            dma((4,)), dma((4,)),
            dma((4,)), dma((4,)),
        ],
        compiler_params=pltpu.CompilerParams(
            collective_id=0, has_side_effects=True, vmem_limit_bytes=48 * 2**20
        ),
    )(hidden_act, out_grad, weight, loss_mask.reshape(-1, 128), positions.reshape(-1, 128))


def solution(mesh):
    return jax.shard_map(
        on_device,
        mesh=mesh,
        in_specs=(P("row", "col"), P("col", "row"), P("col", "row"), P(), P()),
        out_specs=(P("row", "col"), P("col", "row")),
        check_vma=False,
    )
```

time: 300 us -> 80.3 us (0.27)
  waiting for transfers between devices: 243 us -> 0 us
  Pallas kernels: 0 us -> 73.1 us
  local copies, waits for them, and re-layouts: 25.2 us -> 5.95 us
  between operations: 13.8 us -> 0.65 us
  matrix products: 10.8 us -> 0 us
  other arithmetic: 6.82 us -> 0 us
    all_gather x2 -> x0, waiting for transfers between devices: 144 us -> none  [the longest x1 73.1 us: on_device(): scaled_all = lax.all_gather(scaled_local, 'col', axis=0, tiled=True)]
    reduce_scatter x1 -> x0, waiting for transfers between devices: 97.7 us -> none  [on_device(): lax.psum_scatter(partial_sum.astype(jnp.bfloat16), 'row', scatter_dimensi...]
    pallas_call x0 -> x1, Pallas kernels: none -> 73.1 us  [on_device(): pl.pallas_call(kernel, out_shape=(jax.ShapeDtypeStruct((t, f), BF16), jax...]
    gather x2 -> x0, local copies, waits for them, and re-layouts: 23.6 us -> none  [token_weights(): kept_counts = jnp.maximum(kept_prefix[doc_end] - kept_prefix[doc_first], 1)]
    dot_general x2 -> x0, matrix products: 10.8 us -> none  [the longest x1 5.8 us: on_device(): lax.dot_general(scaled_all, weight, (((1,), (1,)), ((), ())), preferred_e...]
    unnamed x5 -> x12, local copies, waits for them, and re-layouts: 1.31 us -> 5.95 us
    another operation x7 -> x0, other arithmetic: 3.62 us -> none
  transfers between devices with their start and end apart: 3 -> 0, of which waited for: 3 -> 0; matrix products, arithmetic and copies ran while one was open for 4% -> 0% of each run, Pallas kernels for 0% -> 0%
where the time goes in v1:
time: 80.3 us; the launch traced here: 79.7 us
  Pallas kernels  73.1 us (91%)
  local copies, waits for them, and re-layouts  5.95 us (7%)
    pallas_call x1, Pallas kernels, on_device(): pl.pallas_call(kernel, out_shape=(jax.ShapeDtypeStruct((t, f), BF16), jax...  73.1 us
    unnamed x12, local copies, waits for them, and re-layouts  5.95 us

profile of v1, /device:TPU:1, one launch (start us, length us, event | category | flops | bytes accessed | tf_op | source)
XLA Modules:
  0.0 79.7 jit_solution(14406653781611908046)
XLA Ops:
  0.6 0.0 copy-start
  0.6 1.2 %copy-done = bf16[896,512]{1,0:T(8,128)(2,1)S(1)} copy-done((bf16[896,512]{1,0:T(8,128)(2,1)S(1)}, bf16[896,512]{1,0:T(8,128)(2,1)}, u32[]{:S(2)}) %copy-start) | copy-done | bytes 917528
  1.8 0.0 copy-start.1
  1.8 0.9 %copy-done.1 = bf16[128,896]{1,0:T(8,128)(2,1)S(1)} copy-done((bf16[128,896]{1,0:T(8,128)(2,1)S(1)}, bf16[128,896]{1,0:T(8,128)(2,1)}, u32[]{:S(2)}) %copy-start.1) | copy-done | bytes 229400
  2.8 0.0 copy-start.2
  2.8 0.8 %copy-done.2 = bf16[64,512]{1,0:T(8,128)(2,1)S(1)} copy-done((bf16[64,512]{1,0:T(8,128)(2,1)S(1)}, bf16[64,512]{1,0:T(8,128)(2,1)}, u32[]{:S(2)}) %copy-start.2) | copy-done | bytes 65560
  3.6 0.0 copy-start.3
  3.6 0.7 copy-done.3
  4.3 0.0 copy-start.4
  4.3 0.7 copy-done.4
  5.0 73.1 %shard_map.68 = (bf16[128,896]{1,0:T(8,128)(2,1)S(1)}, bf16[896,512]{1,0:T(8,128)(2,1)S(1)}) custom-call(bf16[128,896]{1,0:T(8,128)(2,1)S(1)} %copy-done.1, bf16[64,512]{1,0:T(8,128)(2,1)S(1)} %copy-done.2, bf16[896,512]{1,0:T(8,128)(2,1)S(1)} %copy-done, s32[16,128]{1,0:T(8,128)S(1)} %bitcast.2, s32[16,128]{1,0:T(8,128)S(1)} %bitcast.3), custom_call_target="tpu_custom_call" | custom-call | tf_op jit(solution)/shard_map/pallas_call | solution.py:235
  78.1 0.7 copy.9
  78.8 0.9 %copy.10 = bf16[896,512]{1,0:T(8,128)(2,1)} copy(bf16[896,512]{1,0:T(8,128)(2,1)S(1)} %get-tuple-element.5) | data formatting | bytes 1835008
Async XLA Ops:
  0.6 1.2 %copy-start = (bf16[896,512]{1,0:T(8,128)(2,1)S(1)}, bf16[896,512]{1,0:T(8,128)(2,1)}, u32[]{:S(2)}) copy-start(bf16[896,512]{1,0:T(8,128)(2,1)} %w_ref.1) | copy-start | bytes 2752516
  1.8 0.9 %copy-start.1 = (bf16[128,896]{1,0:T(8,128)(2,1)S(1)}, bf16[128,896]{1,0:T(8,128)(2,1)}, u32[]{:S(2)}) copy-start(bf16[128,896]{1,0:T(8,128)(2,1)} %hid_ref.1) | copy-start | bytes 688132
  2.8 0.8 %copy-start.2 = (bf16[64,512]{1,0:T(8,128)(2,1)S(1)}, bf16[64,512]{1,0:T(8,128)(2,1)}, u32[]{:S(2)}) copy-start(bf16[64,512]{1,0:T(8,128)(2,1)} %og_ref.1) | copy-start | bytes 196612
  3.6 0.7 copy-start.3
  4.3 0.7 copy-start.4

commit v2 on v1

v2 whole, which is shorter than its diff:
```python
import contextlib

import jax
import jax.numpy as jnp
from jax import lax
from jax.experimental import pallas as pl
from jax.experimental.pallas import tpu as pltpu
from jax.sharding import PartitionSpec as P

MESH = pl.DeviceIdType.MESH
BF16 = jnp.bfloat16
F32 = jnp.float32
NY, NX, NZ = 4, 4, 8
scope = contextlib.nullcontext
VMEM_LIMIT = 62 * 2**20
SUB = 2
LAST_HF = 4
CH = 4


def local_token_scale(mask_ref, pos_ref, col, n_local):
    rows = pos_ref.shape[0]
    lane = lax.broadcasted_iota(jnp.int32, (n_local, 128), 1)
    sub = lax.broadcasted_iota(jnp.int32, (n_local, 128), 0)
    per = 128 // n_local
    mine_row = col // per
    offset = (col % per) * n_local
    pick = lane == sub + offset
    mine_pos = pos_ref[pl.ds(mine_row, 1), :]
    mine_mask = mask_ref[pl.ds(mine_row, 1), :]
    first = jnp.sum(jnp.where(pick, (mine_row * 128 + lane - mine_pos).astype(F32), 0.0), axis=1, keepdims=True)
    own_mask = jnp.sum(jnp.where(pick, mine_mask.astype(F32), 0.0), axis=1, keepdims=True)
    length = jnp.zeros((n_local, 128), F32)
    kept = jnp.zeros((n_local, 128), F32)
    for q in range(rows):
        begins = (q * 128 + lane - pos_ref[q : q + 1, :]).astype(F32)
        same = begins == first
        length = length + jnp.where(same, 1.0, 0.0)
        kept = kept + jnp.where(same, mask_ref[q : q + 1, :].astype(F32), 0.0)
    length = jnp.sum(length, axis=1, keepdims=True)
    kept = jnp.maximum(jnp.sum(kept, axis=1, keepdims=True), 1.0)
    return own_mask * length / kept


def dot_nn(a, b):
    return lax.dot_general(a, b, (((1,), (0,)), ((), ())), preferred_element_type=F32)


def dot_nt(a, b):
    return lax.dot_general(a, b, (((1,), (1,)), ((), ())), preferred_element_type=F32)


def kernel(
    hid_hbm, og_hbm, w_hbm, mask_hbm, pos_hbm, ig_ref, wg_ref,
    hid_ref, og_ref, w_ref, mask_ref, pos_ref,
    sc, hidt, S, wrecv, wg_send, wg_recv, wg_own, ig_send, ig_recv, ig_own, a_send, a_recv, b_send, b_recv,
    in_s, sc_s, sc_r, hy_s, hy_r, hx_s, hx_r, w_s, w_r, z_s, z_r, k_s, k_r, wg_s, wg_r, ig_s, ig_r, a_s, a_r, b_s, b_r,
):
    row = lax.axis_index("row")
    col = lax.axis_index("col")
    Y, x = row // NX, row % NX
    z, l, k = col // 4, (col // 2) % 2, col % 2
    dpx = x + 1 - 2 * (x % 2)
    tpx = 3 - x
    par, tpar = x // 2, 1 - x // 2
    g = ((x + 1) // 2) % 2
    lt = (z % 2 + g) % 2

    def dev(Y=Y, x=x, z=z, l=l, k=k):
        return (Y * NX + x, z * 4 + l * 2 + k)

    dp, tp, other = dev(x=dpx), dev(x=tpx), dev(k=1 - k)
    zdev = (dev(z=(z + 1) % NZ), dev(z=(z + NZ - 1) % NZ))
    ydev = (dev(Y=(Y + 1) % NY), dev(Y=(Y + NY - 1) % NY))
    ldev, dpl = dev(l=1 - l), dev(x=dpx, l=1 - l)

    bar = pltpu.get_barrier_semaphore()
    peers = [dp, tp, other, *zdev, *ydev, ldev, dpl]
    for p in peers:
        pl.semaphore_signal(bar, inc=1, device_id=p, device_id_type=MESH)
    load = [
        pltpu.make_async_copy(a, b, in_s.at[i])
        for i, (a, b) in enumerate(
            [(mask_hbm, mask_ref), (pos_hbm, pos_ref), (og_hbm, og_ref), (hid_hbm, hid_ref), (w_hbm, w_ref)]
        )
    ]
    for c in load:
        c.start()

    sends = []

    def rc(src, dst, ss, rs, to):
        return pltpu.make_async_remote_copy(src, dst, ss, rs, device_id=to, device_id_type=MESH)

    def go(src, dst, ss, rs, to):
        c = rc(src, dst, ss, rs, to)
        c.start()
        sends.append(c)
        return c

    for c in load[:3]:
        c.wait()
    scale = local_token_scale(mask_ref, pos_ref, col, og_ref.shape[0])
    sc[...] = (og_ref[...].astype(F32) * scale).astype(BF16)
    pl.semaphore_wait(bar, len(peers))

    member = l == lt
    a_far = rc(sc, S.at[z, k, 1], sc_s.at[0], sc_r.at[1], dp)
    b_far = rc(sc, S.at[z, k, 1], sc_s.at[1], sc_r.at[1], dpl)
    b_near = rc(sc, S.at[z, k, 0], sc_s.at[1], sc_r.at[0], ldev)

    @pl.when(member)
    def _():
        b_near.start()
        S[z, k, 0] = sc[...]

    @pl.when(jnp.logical_not(member))
    def _():
        a_far.start()
        b_far.start()

    wc = go(w_hbm, wrecv, w_s.at[0], w_r.at[0], dp)
    myj = 2 * Y + par
    half = hid_ref.shape[1] // 2
    load[3].wait()
    hidt[myj] = hid_ref[...].T

    def hrows(j, h):
        return hidt.at[j, pl.ds(h * half, half)]

    def block_of(d, parity):
        return 2 * ((Y + d) % NY) + parity

    hy, hx, hf = {}, {}, {}

    def send_hx(d, h):
        r = hrows(block_of(d, par), h)
        hx[d, h] = go(r, r, hx_s.at[d * 2 + h], hx_r.at[d * 2 + h], tp)

    for h in range(2):
        for e in range(2):
            hy[e, h] = go(hrows(myj, h), hrows(myj, h), hy_s.at[e * 2 + h], hy_r.at[e * 2 + h], ydev[e])
    send_hx(0, 0)
    send_hx(0, 1)

    def y_arrived(e, h):
        hy[e, h].wait_recv()
        if h == e:
            r = hrows(block_of((NY - 1, 1)[e], par), h)
            hf[e] = go(r, r, hy_s.at[4 + e], hy_r.at[4 + e], ydev[e])
        send_hx((NY - 1, 1)[e], h)

    a_far.wait_recv()

    kc, zc = {}, {}

    def to_core(zz, slot, idx):
        kc[idx, slot] = go(S.at[zz, k, slot], S.at[zz, k, slot], k_s.at[idx * 2 + slot], k_r.at[idx * 2 + slot], other)

    def origin_of(e, step):
        return (z + NZ - step) % NZ if e == 0 else (z + step) % NZ

    part = S.shape[3] // SUB

    def z_send(e, step, slot, u):
        i = ((e * 4 + step) * 2 + slot) * SUB + u
        r = S.at[origin_of(e, step), k, slot, pl.ds(u * part, part)]
        zc[e, step, slot, u] = go(r, r, z_s.at[i], z_r.at[i], zdev[e])

    for slot in (1, 0):
        if slot == 0:

            @pl.when(jnp.logical_not(member))
            def _():
                b_near.wait_recv()

        for u in range(SUB):
            for e in range(2):
                z_send(e, 0, slot, u)
    for slot in (1, 0):
        to_core(z, slot, 0)
    for step in range(1, 5):
        for slot in (1, 0):
            for u in range(SUB):
                for e in range(2):
                    if step == 4 and slot == e:
                        continue
                    zc[e, step - 1, slot, u].wait_recv()
                    if step < 3 or (step == 3 and slot != e):
                        z_send(e, step, slot, u)
                    if u == SUB - 1:
                        to_core(origin_of(e, step), slot, step if e == 0 or step == 4 else 4 + step)
        if step == 1:
            y_arrived(0, 0)
            y_arrived(1, 0)
        if step == 2:
            y_arrived(0, 1)
            y_arrived(1, 1)
        if step == LAST_HF:
            for e in range(2):
                hf[e].wait_recv()
                send_hx(2, e)
    for slot in (1, 0):
        for i in range(8):
            kc[i, slot].wait_recv()

    load[4].wait()
    wc.wait_recv()

    def ig_block(d, parity):
        zz = block_of(d, parity)
        s0 = S[zz, :, 0].reshape(128, -1)
        s1 = S[zz, :, 1].reshape(128, -1)
        return dot_nt(s0, w_ref[...]) + dot_nt(s1, wrecv[...])

    igc, wgc = {}, {}

    def ig_partner(d):
        with scope(f"igp{d}"):
            ig_send[d] = ig_block(d, tpar).astype(BF16)

    def send_ig(d, h):
        r = pl.ds(h * 64, 64)
        igc[d, h] = go(ig_send.at[d, r], ig_recv.at[d, r], ig_s.at[d * 2 + h], ig_r.at[d * 2 + h], tp)

    rows = hid_ref.shape[1] // CH

    def lhs(c):
        return jnp.concatenate([hidt[j, c * rows : (c + 1) * rows] for j in range(2 * NY)], axis=1)

    def rhs(slot):
        return S[:, :, slot].reshape(1024, -1)

    def wg_partner(c):
        sl = pl.ds(c * rows, rows)
        with scope(f"wgp{c}"):
            wg_send[sl] = dot_nn(lhs(c), rhs(1)).astype(BF16)
        wgc[c] = go(wg_send.at[sl], wg_recv.at[sl], wg_s.at[c], wg_r.at[c], dp)

    ig_partner(2)
    send_ig(2, 0)
    send_ig(2, 1)
    for d in range(NY):
        hx[d, 0].wait_recv()
    for c in range(CH // 2):
        wg_partner(c)
    ig_partner(1)
    send_ig(1, 1)
    ig_partner(3)
    send_ig(3, 0)
    send_ig(1, 0)
    send_ig(3, 1)
    for d in range(NY):
        hx[d, 1].wait_recv()
    for c in range(CH // 2, CH):
        wg_partner(c)
    ig_partner(0)
    send_ig(0, 0)
    send_ig(0, 1)
    for d in (2, 1, 3, 0):
        ig_own[d] = ig_block(d, par)
    for c in range(CH):
        wg_own[c * rows : (c + 1) * rows] = dot_nn(lhs(c), rhs(0))

    ac, bc = {}, {}

    def arrived(d, h):
        igc[d, h].wait_recv()
        r = pl.ds(h * 64, 64)
        return ig_own[d, r] + ig_recv[d, r].astype(F32)

    def send_b(e, h, value):
        r = pl.ds(h * 64, 64)
        b_send[e, r] = value.astype(BF16)
        bc[e, h] = go(b_send.at[e, r], b_recv.at[e, r], b_s.at[e * 2 + h], b_r.at[e * 2 + h], ydev[e])

    def wg_done(c):
        wgc[c].wait_recv()
        sl = pl.ds(c * rows, rows)
        wg_ref[sl] = (wg_own[sl] + wg_recv[sl].astype(F32)).astype(BF16)

    for e in range(2):
        a_send[e] = arrived(2, e).astype(BF16)
        ac[e] = go(a_send.at[e], a_recv.at[e], a_s.at[e], a_r.at[e], ydev[e])
    send_b(0, 1, arrived(1, 1))
    send_b(1, 0, arrived(3, 0))
    t = arrived(1, 0)
    ac[0].wait_recv()
    send_b(0, 0, t + a_recv[0].astype(F32))
    t = arrived(3, 1)
    ac[1].wait_recv()
    send_b(1, 1, t + a_recv[1].astype(F32))
    for c in range(CH - 1):
        wg_done(c)
    for h in range(2):
        ig_own[0, h * 64 : (h + 1) * 64] = arrived(0, h)
    wg_done(CH - 1)
    for h in range(2):
        for e in range(2):
            bc[e, h].wait_recv()
        r = pl.ds(h * 64, 64)
        ig_ref[r] = (ig_own[0, r] + b_recv[0, r].astype(F32) + b_recv[1, r].astype(F32)).astype(BF16)

    b_near.wait_send()

    @pl.when(jnp.logical_not(member))
    def _():
        a_far.wait_send()

    for c in sends:
        c.wait_send()


def on_device(hidden_act, out_grad, weight, loss_mask, positions):
    t, f = hidden_act.shape
    n, b = out_grad.shape
    dma = pltpu.SemaphoreType.DMA
    vm = pltpu.VMEM
    return pl.pallas_call(
        kernel,
        out_shape=(pltpu.VMEM((t, f), BF16), pltpu.VMEM((f, b), BF16)),
        in_specs=[pl.BlockSpec(memory_space=pl.ANY)] * 5,
        out_specs=[pl.BlockSpec(memory_space=vm)] * 2,
        scratch_shapes=[
            vm((t, f), BF16),
            vm((n, b), BF16),
            vm((f, b), BF16),
            vm((16, 128), jnp.int32),
            vm((16, 128), jnp.int32),
            vm((n, b), BF16),
            vm((8, f, t), BF16),
            vm((NZ, 2, 2, n, b), BF16),
            vm((f, b), BF16),
            vm((f, b), BF16),
            vm((f, b), BF16),
            vm((f, b), F32),
            vm((NY, t, f), BF16),
            vm((NY, t, f), BF16),
            vm((NY, t, f), F32),
            vm((2, t // 2, f), BF16),
            vm((2, t // 2, f), BF16),
            vm((2, t, f), BF16),
            vm((2, t, f), BF16),
            dma((5,)),
            dma((2,)), dma((2,)),
            dma((6,)), dma((6,)),
            dma((8,)), dma((8,)),
            dma((1,)), dma((1,)),
            dma((16 * SUB,)), dma((16 * SUB,)),
            dma((16,)), dma((16,)),
            dma((CH,)), dma((CH,)),
            dma((8,)), dma((8,)),
            dma((2,)), dma((2,)),
            dma((4,)), dma((4,)),
        ],
        compiler_params=pltpu.CompilerParams(
            collective_id=0, has_side_effects=True, vmem_limit_bytes=VMEM_LIMIT
        ),
    )(hidden_act, out_grad, weight, loss_mask.reshape(-1, 128), positions.reshape(-1, 128))


def solution(mesh):
    return jax.shard_map(
        on_device,
        mesh=mesh,
        in_specs=(P("row", "col"), P("col", "row"), P("col", "row"), P(), P()),
        out_specs=(P("row", "col"), P("col", "row")),
        check_vma=False,
    )
```

time: 80.3 us -> 68.6 us (0.85)
  the two profiles are of different devices: /device:TPU:1 before, /device:TPU:10 now
where the time goes in v2:
time: 68.6 us; the launch traced here: 68.5 us
  Pallas kernels  66.2 us (97%)
  local copies, waits for them, and re-layouts  1.61 us (2%)
    pallas_call x1, Pallas kernels, on_device(): pl.pallas_call(kernel, out_shape=(pltpu.VMEM((t, f), BF16), pltpu.VMEM((f...  66.2 us
    unnamed x2, local copies, waits for them, and re-layouts  1.61 us

profile of v2, /device:TPU:10, one launch (start us, length us, event | category | flops | bytes accessed | tf_op | source)
XLA Modules:
  0.0 68.5 jit_solution(12098554170953179992)
XLA Ops:
  0.6 66.2 %shard_map.68 = (bf16[128,896]{1,0:T(8,128)(2,1)S(1)}, bf16[896,512]{1,0:T(8,128)(2,1)S(1)}) custom-call(bf16[128,896]{1,0:T(8,128)(2,1)} %hid_hbm.1, bf16[64,512]{1,0:T(8,128)(2,1)} %og_hbm.1, bf16[896,512]{1,0:T(8,128)(2,1)} %w_hbm.1, s32[16,128]{1,0:T(8,128)} %bitcast.2, s32[16,128]{1,0:T(8,128)} %bitcast.3), custom_call_target="tpu_custom_call" | custom-call | tf_op jit(solution)/shard_map/pallas_call | solution.py:319
  66.8 0.7 %copy.9 = bf16[128,896]{1,0:T(8,128)(2,1)} copy(bf16[128,896]{1,0:T(8,128)(2,1)S(1)} %get-tuple-element.2) | data formatting | bytes 458752
  67.5 0.9 %copy.10 = bf16[896,512]{1,0:T(8,128)(2,1)} copy(bf16[896,512]{1,0:T(8,128)(2,1)S(1)} %get-tuple-element.3) | data formatting | bytes 1835008

commit v3 on v2

--- a/solution.py
+++ b/solution.py
@@ -13,8 +13,7 @@
 NY, NX, NZ = 4, 4, 8
 scope = contextlib.nullcontext
 VMEM_LIMIT = 62 * 2**20
-SUB = 2
-LAST_HF = 4
+YPOS = (1, 2, 4)
 CH = 4
 
 
@@ -71,11 +70,12 @@
 
     dp, tp, other = dev(x=dpx), dev(x=tpx), dev(k=1 - k)
     zdev = (dev(z=(z + 1) % NZ), dev(z=(z + NZ - 1) % NZ))
+    zdev2 = (dev(z=(z + 2) % NZ), dev(z=(z + NZ - 2) % NZ))
     ydev = (dev(Y=(Y + 1) % NY), dev(Y=(Y + NY - 1) % NY))
     ldev, dpl = dev(l=1 - l), dev(x=dpx, l=1 - l)
 
     bar = pltpu.get_barrier_semaphore()
-    peers = [dp, tp, other, *zdev, *ydev, ldev, dpl]
+    peers = [dp, tp, other, *zdev, *zdev2, *ydev, ldev, dpl]
     for p in peers:
         pl.semaphore_signal(bar, inc=1, device_id=p, device_id_type=MESH)
     load = [
@@ -137,11 +137,12 @@
         r = hrows(block_of(d, par), h)
         hx[d, h] = go(r, r, hx_s.at[d * 2 + h], hx_r.at[d * 2 + h], tp)
 
-    for h in range(2):
+    def send_own(h):
         for e in range(2):
             hy[e, h] = go(hrows(myj, h), hrows(myj, h), hy_s.at[e * 2 + h], hy_r.at[e * 2 + h], ydev[e])
-    send_hx(0, 0)
-    send_hx(0, 1)
+        send_hx(0, h)
+
+    send_own(0)
 
     def y_arrived(e, h):
         hy[e, h].wait_recv()
@@ -160,12 +161,20 @@
     def origin_of(e, step):
         return (z + NZ - step) % NZ if e == 0 else (z + step) % NZ
 
-    part = S.shape[3] // SUB
-
-    def z_send(e, step, slot, u):
-        i = ((e * 4 + step) * 2 + slot) * SUB + u
-        r = S.at[origin_of(e, step), k, slot, pl.ds(u * part, part)]
-        zc[e, step, slot, u] = go(r, r, z_s.at[i], z_r.at[i], zdev[e])
+    def hidden_step(i):
+        for n in range(len(YPOS)):
+            if YPOS[n] == i:
+                if n < 2:
+                    y_arrived(0, n)
+                    y_arrived(1, n)
+                else:
+                    hf[0].wait_recv()
+                    send_hx(2, 0)
+
+    def z_hop(e, origin_step, sem_step, slot, to):
+        i = (e * 4 + sem_step) * 2 + slot
+        r = S.at[origin_of(e, origin_step), k, slot]
+        zc[e, sem_step, slot] = go(r, r, z_s.at[i], z_r.at[i], to)
 
     for slot in (1, 0):
         if slot == 0:
@@ -174,32 +183,42 @@
             def _():
                 b_near.wait_recv()
 
-        for u in range(SUB):
-            for e in range(2):
-                z_send(e, 0, slot, u)
+        for e in range(2):
+            z_hop(e, 0, 0, slot, zdev[e])
+    for slot in (1, 0):
+        for e in range(2):
+            z_hop(e, 0, 1, slot, zdev2[e])
+    send_own(1)
     for slot in (1, 0):
         to_core(z, slot, 0)
-    for step in range(1, 5):
-        for slot in (1, 0):
-            for u in range(SUB):
-                for e in range(2):
-                    if step == 4 and slot == e:
-                        continue
-                    zc[e, step - 1, slot, u].wait_recv()
-                    if step < 3 or (step == 3 and slot != e):
-                        z_send(e, step, slot, u)
-                    if u == SUB - 1:
-                        to_core(origin_of(e, step), slot, step if e == 0 or step == 4 else 4 + step)
-        if step == 1:
-            y_arrived(0, 0)
-            y_arrived(1, 0)
-        if step == 2:
-            y_arrived(0, 1)
-            y_arrived(1, 1)
-        if step == LAST_HF:
-            for e in range(2):
-                hf[e].wait_recv()
-                send_hx(2, e)
+    for slot in (1, 0):
+        for e in range(2):
+            zc[e, 0, slot].wait_recv()
+            to_core(origin_of(e, 1), slot, 1 if e == 0 else 5)
+    hidden_step(1)
+    for slot in (1, 0):
+        for e in range(2):
+            zc[e, 1, slot].wait_recv()
+            z_hop(e, 2, 2, slot, zdev[e])
+            if slot != e:
+                z_hop(e, 2, 3, slot, zdev2[e])
+            to_core(origin_of(e, 2), slot, 2 if e == 0 else 6)
+        if slot == 1:
+            hidden_step(2)
+    hidden_step(3)
+    for slot in (1, 0):
+        for e in range(2):
+            zc[e, 2, slot].wait_recv()
+            to_core(origin_of(e, 3), slot, 3 if e == 0 else 7)
+        if slot == 1:
+            hidden_step(4)
+    hidden_step(5)
+    hf[1].wait_recv()
+    send_hx(2, 1)
+    for slot in (1, 0):
+        zc[1 - slot, 3, slot].wait_recv()
+        to_core(origin_of(1 - slot, 4), slot, 4)
+    hidden_step(6)
     for slot in (1, 0):
         for i in range(8):
             kc[i, slot].wait_recv()
@@ -219,9 +238,9 @@
         with scope(f"igp{d}"):
             ig_send[d] = ig_block(d, tpar).astype(BF16)
 
-    def send_ig(d, h):
-        r = pl.ds(h * 64, 64)
-        igc[d, h] = go(ig_send.at[d, r], ig_recv.at[d, r], ig_s.at[d * 2 + h], ig_r.at[d * 2 + h], tp)
+    def send_ig(d, q):
+        r = pl.ds(q * 32, 32)
+        igc[d, q] = go(ig_send.at[d, r], ig_recv.at[d, r], ig_s.at[d * 4 + q], ig_r.at[d * 4 + q], tp)
 
     rows = hid_ref.shape[1] // CH
 
@@ -237,69 +256,80 @@
             wg_send[sl] = dot_nn(lhs(c), rhs(1)).astype(BF16)
         wgc[c] = go(wg_send.at[sl], wg_recv.at[sl], wg_s.at[c], wg_r.at[c], dp)
 
+    ac, bc = {}, {}
+
+    def arrived(d, q):
+        igc[d, q].wait_recv()
+        r = pl.ds(q * 32, 32)
+        return ig_own[d, r] + ig_recv[d, r].astype(F32)
+
+    def send_a(q):
+        a_send[q] = arrived(2, q).astype(BF16)
+        ac[q] = go(a_send.at[q], a_recv.at[q], a_s.at[q], a_r.at[q], ydev[q // 2])
+
+    def send_b(d, q):
+        e = d // 2
+        r = pl.ds(q * 32, 32)
+        value = arrived(d, q)
+        if q // 2 == e:
+            ac[q].wait_recv()
+            value = value + a_recv[q].astype(F32)
+        b_send[e, r] = value.astype(BF16)
+        bc[e, q] = go(b_send.at[e, r], b_recv.at[e, r], b_s.at[e * 4 + q], b_r.at[e * 4 + q], ydev[e])
+
+    def ig_own_block(d):
+        ig_own[d] = ig_block(d, par)
+
+    def wg_own_chunk(c):
+        wg_own[c * rows : (c + 1) * rows] = dot_nn(lhs(c), rhs(0))
+
+    def wg_done(c):
+        wgc[c].wait_recv()
+        sl = pl.ds(c * rows, rows)
+        wg_ref[sl] = (wg_own[sl] + wg_recv[sl].astype(F32)).astype(BF16)
+
     ig_partner(2)
-    send_ig(2, 0)
-    send_ig(2, 1)
+    for q in (0, 2, 1, 3):
+        send_ig(2, q)
     for d in range(NY):
         hx[d, 0].wait_recv()
     for c in range(CH // 2):
         wg_partner(c)
     ig_partner(1)
-    send_ig(1, 1)
     ig_partner(3)
-    send_ig(3, 0)
-    send_ig(1, 0)
-    send_ig(3, 1)
+    for d, q in ((1, 2), (3, 0), (1, 3), (3, 1), (1, 0), (3, 2), (1, 1), (3, 3)):
+        send_ig(d, q)
+    ig_own_block(2)
+    ig_partner(0)
+    for q in range(4):
+        send_ig(0, q)
+    ig_own_block(1)
+    ig_own_block(3)
+    for q in (0, 2, 1, 3):
+        send_a(q)
+    send_b(1, 2)
+    send_b(3, 0)
     for d in range(NY):
         hx[d, 1].wait_recv()
     for c in range(CH // 2, CH):
         wg_partner(c)
-    ig_partner(0)
-    send_ig(0, 0)
-    send_ig(0, 1)
-    for d in (2, 1, 3, 0):
-        ig_own[d] = ig_block(d, par)
+    send_b(1, 3)
+    send_b(3, 1)
+    ig_own_block(0)
     for c in range(CH):
-        wg_own[c * rows : (c + 1) * rows] = dot_nn(lhs(c), rhs(0))
-
-    ac, bc = {}, {}
-
-    def arrived(d, h):
-        igc[d, h].wait_recv()
-        r = pl.ds(h * 64, 64)
-        return ig_own[d, r] + ig_recv[d, r].astype(F32)
-
-    def send_b(e, h, value):
-        r = pl.ds(h * 64, 64)
-        b_send[e, r] = value.astype(BF16)
-        bc[e, h] = go(b_send.at[e, r], b_recv.at[e, r], b_s.at[e * 2 + h], b_r.at[e * 2 + h], ydev[e])
-
-    def wg_done(c):
-        wgc[c].wait_recv()
-        sl = pl.ds(c * rows, rows)
-        wg_ref[sl] = (wg_own[sl] + wg_recv[sl].astype(F32)).astype(BF16)
-
-    for e in range(2):
-        a_send[e] = arrived(2, e).astype(BF16)
-        ac[e] = go(a_send.at[e], a_recv.at[e], a_s.at[e], a_r.at[e], ydev[e])
-    send_b(0, 1, arrived(1, 1))
-    send_b(1, 0, arrived(3, 0))
-    t = arrived(1, 0)
-    ac[0].wait_recv()
-    send_b(0, 0, t + a_recv[0].astype(F32))
-    t = arrived(3, 1)
-    ac[1].wait_recv()
-    send_b(1, 1, t + a_recv[1].astype(F32))
+        wg_own_chunk(c)
+    for q in range(2):
+        send_b(1, q)
+        send_b(3, 2 + q)
     for c in range(CH - 1):
         wg_done(c)
-    for h in range(2):
-        ig_own[0, h * 64 : (h + 1) * 64] = arrived(0, h)
+    for q in range(4):
+        ig_own[0, q * 32 : (q + 1) * 32] = arrived(0, q)
     wg_done(CH - 1)
-    for h in range(2):
-        for e in range(2):
-            bc[e, h].wait_recv()
-        r = pl.ds(h * 64, 64)
-        ig_ref[r] = (ig_own[0, r] + b_recv[0, r].astype(F32) + b_recv[1, r].astype(F32)).astype(BF16)
+    for q in (2, 3, 0, 1):
+        for e in range(2):
+            bc[e, q].wait_recv()
+    ig_ref[...] = (ig_own[0] + b_recv[0].astype(F32) + b_recv[1].astype(F32)).astype(BF16)
 
     b_near.wait_send()
 
@@ -337,8 +367,8 @@
             vm((NY, t, f), BF16),
             vm((NY, t, f), BF16),
             vm((NY, t, f), F32),
-            vm((2, t // 2, f), BF16),
-            vm((2, t // 2, f), BF16),
+            vm((4, t // 4, f), BF16),
+            vm((4, t // 4, f), BF16),
             vm((2, t, f), BF16),
             vm((2, t, f), BF16),
             dma((5,)),
@@ -346,12 +376,12 @@
             dma((6,)), dma((6,)),
             dma((8,)), dma((8,)),
             dma((1,)), dma((1,)),
-            dma((16 * SUB,)), dma((16 * SUB,)),
+            dma((16,)), dma((16,)),
             dma((16,)), dma((16,)),
             dma((CH,)), dma((CH,)),
+            dma((16,)), dma((16,)),
+            dma((4,)), dma((4,)),
             dma((8,)), dma((8,)),
-            dma((2,)), dma((2,)),
-            dma((4,)), dma((4,)),
         ],
         compiler_params=pltpu.CompilerParams(
             collective_id=0, has_side_effects=True, vmem_limit_bytes=VMEM_LIMIT

time: 68.6 us -> 66.7 us (0.972)
  Pallas kernels: 66.2 us -> 64.3 us
    pallas_call x1, Pallas kernels: 66.2 us -> 64.3 us  [on_device(): pl.pallas_call(kernel, out_shape=(pltpu.VMEM((t, f), BF16), pltpu.VMEM((f...]
where the time goes in v3:
time: 66.7 us; the launch traced here: 66.5 us
  Pallas kernels  64.3 us (96%)
  local copies, waits for them, and re-layouts  1.61 us (2%)
    pallas_call x1, Pallas kernels, on_device(): pl.pallas_call(kernel, out_shape=(pltpu.VMEM((t, f), BF16), pltpu.VMEM((f...  64.3 us
    unnamed x2, local copies, waits for them, and re-layouts  1.61 us

profile of v3, /device:TPU:10, one launch (start us, length us, event | category | flops | bytes accessed | tf_op | source)
XLA Modules:
  0.0 66.5 jit_solution(6874369550402126792)
XLA Ops:
  0.6 64.3 %shard_map.68 = (bf16[128,896]{1,0:T(8,128)(2,1)S(1)}, bf16[896,512]{1,0:T(8,128)(2,1)S(1)}) custom-call(bf16[128,896]{1,0:T(8,128)(2,1)} %hid_hbm.1, bf16[64,512]{1,0:T(8,128)(2,1)} %og_hbm.1, bf16[896,512]{1,0:T(8,128)(2,1)} %w_hbm.1, s32[16,128]{1,0:T(8,128)} %bitcast.2, s32[16,128]{1,0:T(8,128)} %bitcast.3), custom_call_target="tpu_custom_call" | custom-call | tf_op jit(solution)/shard_map/pallas_call | solution.py:349
  64.9 0.7 %copy.9 = bf16[128,896]{1,0:T(8,128)(2,1)} copy(bf16[128,896]{1,0:T(8,128)(2,1)S(1)} %get-tuple-element.2) | data formatting | bytes 458752
  65.6 0.9 %copy.10 = bf16[896,512]{1,0:T(8,128)(2,1)} copy(bf16[896,512]{1,0:T(8,128)(2,1)S(1)} %get-tuple-element.3) | data formatting | bytes 1835008

commit v4 on v3

--- a/solution.py
+++ b/solution.py
@@ -13,7 +13,9 @@
 NY, NX, NZ = 4, 4, 8
 scope = contextlib.nullcontext
 VMEM_LIMIT = 62 * 2**20
-YPOS = (1, 2, 4)
+YPOS = (1, 2, 4, 5)
+YPOS_EARLY = (0, 0, 0, 0)
+EARLY = 1
 CH = 4
 
 
@@ -53,7 +55,7 @@
     hid_hbm, og_hbm, w_hbm, mask_hbm, pos_hbm, ig_ref, wg_ref,
     hid_ref, og_ref, w_ref, mask_ref, pos_ref,
     sc, hidt, S, wrecv, wg_send, wg_recv, wg_own, ig_send, ig_recv, ig_own, a_send, a_recv, b_send, b_recv,
-    in_s, sc_s, sc_r, hy_s, hy_r, hx_s, hx_r, w_s, w_r, z_s, z_r, k_s, k_r, wg_s, wg_r, ig_s, ig_r, a_s, a_r, b_s, b_r,
+    in_s, z_in, sc_s, sc_r, hy_s, hy_r, hx_s, hx_r, w_s, w_r, z_s, z_r, k_s, k_r, wg_s, wg_r, ig_s, ig_r, a_s, a_r, b_s, b_r,
 ):
     row = lax.axis_index("row")
     col = lax.axis_index("col")
@@ -75,9 +77,16 @@
     ldev, dpl = dev(l=1 - l), dev(x=dpx, l=1 - l)
 
     bar = pltpu.get_barrier_semaphore()
-    peers = [dp, tp, other, *zdev, *zdev2, *ydev, ldev, dpl]
+    peers = [dp, tp, other, *ydev, ldev, dpl]
     for p in peers:
         pl.semaphore_signal(bar, inc=1, device_id=p, device_id_type=MESH)
+    zpeers = [(z + step) % NZ for step in (1, NZ - 1, 2, NZ - 2)]
+    for zz in zpeers:
+
+        @pl.when(zz > z)
+        def _():
+            pl.semaphore_signal(bar, inc=1, device_id=dev(z=zz), device_id_type=MESH)
+
     load = [
         pltpu.make_async_copy(a, b, in_s.at[i])
         for i, (a, b) in enumerate(
@@ -102,7 +111,14 @@
         c.wait()
     scale = local_token_scale(mask_ref, pos_ref, col, og_ref.shape[0])
     sc[...] = (og_ref[...].astype(F32) * scale).astype(BF16)
-    pl.semaphore_wait(bar, len(peers))
+    below = sum(((zz < z).astype(jnp.int32) for zz in zpeers), 0)
+    pl.semaphore_wait(bar, len(peers) + below)
+    for zz in zpeers:
+
+        @pl.when(zz < z)
+        def _():
+            pl.semaphore_signal(z_in, inc=1, device_id=dev(z=zz), device_id_type=MESH)
+
 
     member = l == lt
     a_far = rc(sc, S.at[z, k, 1], sc_s.at[0], sc_r.at[1], dp)
@@ -133,9 +149,17 @@
 
     hy, hx, hf = {}, {}, {}
 
+    for d in range(NY):
+        for h in range(2):
+            r = hrows(block_of(d, par), h)
+            hx[d, h] = rc(r, r, hx_s.at[d * 2 + h], hx_r.at[d * 2 + h], tp)
+    for e in range(2):
+        r = hrows(block_of((NY - 1, 1)[e], par), e)
+        hf[e] = rc(r, r, hy_s.at[4 + e], hy_r.at[4 + e], ydev[e])
+    sends.extend([*hx.values(), *hf.values()])
+
     def send_hx(d, h):
-        r = hrows(block_of(d, par), h)
-        hx[d, h] = go(r, r, hx_s.at[d * 2 + h], hx_r.at[d * 2 + h], tp)
+        hx[d, h].start()
 
     def send_own(h):
         for e in range(2):
@@ -147,9 +171,8 @@
     def y_arrived(e, h):
         hy[e, h].wait_recv()
         if h == e:
-            r = hrows(block_of((NY - 1, 1)[e], par), h)
-            hf[e] = go(r, r, hy_s.at[4 + e], hy_r.at[4 + e], ydev[e])
-        send_hx((NY - 1, 1)[e], h)
+            hf[e].start()
+        hx[(NY - 1, 1)[e], h].start()
 
     a_far.wait_recv()
 
@@ -162,20 +185,31 @@
         return (z + NZ - step) % NZ if e == 0 else (z + step) % NZ
 
     def hidden_step(i):
-        for n in range(len(YPOS)):
-            if YPOS[n] == i:
-                if n < 2:
-                    y_arrived(0, n)
-                    y_arrived(1, n)
-                else:
-                    hf[0].wait_recv()
-                    send_hx(2, 0)
+        for places, here in ((YPOS, z >= EARLY), (YPOS_EARLY, z < EARLY)):
+            if i not in places:
+                continue
+
+            @pl.when(here)
+            def _():
+                for n in range(4):
+                    if places[n] != i:
+                        continue
+                    if n < 2:
+                        y_arrived(0, n)
+                        y_arrived(1, n)
+                    else:
+                        hf[n - 2].wait_recv()
+                        send_hx(2, n - 2)
 
     def z_hop(e, origin_step, sem_step, slot, to):
         i = (e * 4 + sem_step) * 2 + slot
         r = S.at[origin_of(e, origin_step), k, slot]
         zc[e, sem_step, slot] = go(r, r, z_s.at[i], z_r.at[i], to)
 
+    @pl.when(below < len(zpeers))
+    def _():
+        pl.semaphore_wait(z_in, len(zpeers) - below)
+
     for slot in (1, 0):
         if slot == 0:
 
@@ -191,6 +225,7 @@
     send_own(1)
     for slot in (1, 0):
         to_core(z, slot, 0)
+    hidden_step(0)
     for slot in (1, 0):
         for e in range(2):
             zc[e, 0, slot].wait_recv()
@@ -213,8 +248,6 @@
         if slot == 1:
             hidden_step(4)
     hidden_step(5)
-    hf[1].wait_recv()
-    send_hx(2, 1)
     for slot in (1, 0):
         zc[1 - slot, 3, slot].wait_recv()
         to_core(origin_of(1 - slot, 4), slot, 4)
@@ -372,6 +405,7 @@
             vm((2, t, f), BF16),
             vm((2, t, f), BF16),
             dma((5,)),
+            pltpu.SemaphoreType.REGULAR,
             dma((2,)), dma((2,)),
             dma((6,)), dma((6,)),
             dma((8,)), dma((8,)),

time: 66.7 us -> 64.5 us (0.967)
  the two profiles are of different devices: /device:TPU:10 before, /device:TPU:1 now
where the time goes in v4:
time: 64.5 us; the launch traced here: 64.4 us
  Pallas kernels  62.1 us (96%)
  local copies, waits for them, and re-layouts  1.61 us (2%)
    pallas_call x1, Pallas kernels, on_device(): pl.pallas_call(kernel, out_shape=(pltpu.VMEM((t, f), BF16), pltpu.VMEM((f...  62.1 us
    unnamed x2, local copies, waits for them, and re-layouts  1.61 us

profile of v4, /device:TPU:1, one launch (start us, length us, event | category | flops | bytes accessed | tf_op | source)
XLA Modules:
  0.0 64.4 jit_solution(12557400012135014551)
XLA Ops:
  0.6 62.1 %shard_map.68 = (bf16[128,896]{1,0:T(8,128)(2,1)S(1)}, bf16[896,512]{1,0:T(8,128)(2,1)S(1)}) custom-call(bf16[128,896]{1,0:T(8,128)(2,1)} %hid_hbm.1, bf16[64,512]{1,0:T(8,128)(2,1)} %og_hbm.1, bf16[896,512]{1,0:T(8,128)(2,1)} %w_hbm.1, s32[16,128]{1,0:T(8,128)} %bitcast.2, s32[16,128]{1,0:T(8,128)} %bitcast.3), custom_call_target="tpu_custom_call" | custom-call | tf_op jit(solution)/shard_map/pallas_call | solution.py:382
  62.7 0.7 %copy.9 = bf16[128,896]{1,0:T(8,128)(2,1)} copy(bf16[128,896]{1,0:T(8,128)(2,1)S(1)} %get-tuple-element.2) | data formatting | bytes 458752
  63.4 0.9 %copy.10 = bf16[896,512]{1,0:T(8,128)(2,1)} copy(bf16[896,512]{1,0:T(8,128)(2,1)S(1)} %get-tuple-element.3) | data formatting | bytes 1835008

commit v5 on v4

--- a/solution.py
+++ b/solution.py
@@ -13,7 +13,7 @@
 NY, NX, NZ = 4, 4, 8
 scope = contextlib.nullcontext
 VMEM_LIMIT = 62 * 2**20
-YPOS = (1, 2, 4, 5)
+YPOS = (1, 1, 3, 4)
 YPOS_EARLY = (0, 0, 0, 0)
 EARLY = 1
 CH = 4

time: 64.5 us -> 65.6 us (1.017)
  Pallas kernels: 62.1 us -> 63.2 us
    pallas_call x1, Pallas kernels: 62.1 us -> 63.2 us  [on_device(): pl.pallas_call(kernel, out_shape=(pltpu.VMEM((t, f), BF16), pltpu.VMEM((f...]
where the time goes in v5:
time: 65.6 us; the launch traced here: 65.4 us
  Pallas kernels  63.2 us (96%)
  local copies, waits for them, and re-layouts  1.61 us (2%)
    pallas_call x1, Pallas kernels, on_device(): pl.pallas_call(kernel, out_shape=(pltpu.VMEM((t, f), BF16), pltpu.VMEM((f...  63.2 us
    unnamed x2, local copies, waits for them, and re-layouts  1.61 us

profile of v5, /device:TPU:1, one launch (start us, length us, event | category | flops | bytes accessed | tf_op | source)
XLA Modules:
  0.0 65.4 jit_solution(11080404781085741957)
XLA Ops:
  0.6 63.2 %shard_map.68 = (bf16[128,896]{1,0:T(8,128)(2,1)S(1)}, bf16[896,512]{1,0:T(8,128)(2,1)S(1)}) custom-call(bf16[128,896]{1,0:T(8,128)(2,1)} %hid_hbm.1, bf16[64,512]{1,0:T(8,128)(2,1)} %og_hbm.1, bf16[896,512]{1,0:T(8,128)(2,1)} %w_hbm.1, s32[16,128]{1,0:T(8,128)} %bitcast.2, s32[16,128]{1,0:T(8,128)} %bitcast.3), custom_call_target="tpu_custom_call" | custom-call | tf_op jit(solution)/shard_map/pallas_call | solution.py:382
  63.8 0.7 %copy.9 = bf16[128,896]{1,0:T(8,128)(2,1)} copy(bf16[128,896]{1,0:T(8,128)(2,1)S(1)} %get-tuple-element.2) | data formatting | bytes 458752
  64.5 0.9 %copy.10 = bf16[896,512]{1,0:T(8,128)(2,1)} copy(bf16[896,512]{1,0:T(8,128)(2,1)S(1)} %get-tuple-element.3) | data formatting | bytes 1835008
